TPU v7x, 256 devices: a whole 4x4x8 slice. The times are simulated.
256 devices in a mesh: dp: 8 (over x, y_hi), expert: 32 (over z, y_lo, core).
Axes of the slice: x: 4, y: 4 (y_hi: 2, y_lo: 2; y = y_hi * 2 + y_lo), z: 8, core: 2. Of those that a mesh axis runs over, the one named last changes fastest.
Arguments:
- tokens: bfloat16 [3072, 4096], P(('dp', 'expert')), may hold values from -6 to 6
- expert_ids: int32 [3072, 8], P(('dp', 'expert')), may hold values from 0 to 63, all different within a row; in each aligned block of 12 rows (0 to 11, 12 to 23, ...) at most 3 rows name the same one
- gate_probs: float32 [3072, 8], P(('dp', 'expert')), may hold values from 0.02 to 5
- in_weight: bfloat16 [64, 4096, 3072], P('expert', None, 'dp'), may hold values from -0.09375 to 0.09375
- out_weight: bfloat16 [64, 1536, 4096], P('expert', 'dp'), may hold values from -0.15625 to 0.15625
- swap_slot: int32 [32], replicated, may hold values from 0 to 1
Outputs:
- mixed_out: bfloat16 [3072, 4096], P(('dp', 'expert'))
- owner_load: float32 [32], replicated
Inputs may be any that keep to these rules, and one draw needn't show every extreme that they name: `expert_ids`: among the rows of one device no expert is named more than 3 times, and in every draw some device's rows name some expert exactly 3 times; a row names 8 different experts.
All inputs are finite; a program needn't handle non-finite values.
Results may differ from a plain program's by a relative error of at most 0.018.
Values may be sent and summed in bfloat16 or wider, within the bound.
A program may use at most 128 MiB of HBM per device.

v0:
```python
import jax
import jax.numpy as jnp
from jax import lax
from jax.sharding import PartitionSpec as P

BOTH = ("dp", "expert")


def planned_load(mass, swap_slot, per_device, owners, tokens_all):
    experts = jnp.arange(mass.shape[0], dtype=jnp.int32)
    home, within = experts // per_device, experts % per_device
    slot = jnp.repeat(swap_slot, per_device)
    holder = jnp.where(within == slot, (home + owners // 2) % owners, home)
    hot = holder[:, None] == jnp.arange(owners, dtype=jnp.int32)
    return jnp.sum(jnp.where(hot, mass[:, None], 0.0), 0) * (owners / tokens_all)


def on_device(tokens, expert_ids, gate_probs, in_weight, out_weight, swap_slot):
    owners = lax.axis_size("expert")
    per_device, width = in_weight.shape[:2]
    half = out_weight.shape[1]
    experts_all = per_device * owners
    experts = jnp.arange(experts_all, dtype=jnp.int32)
    dense = jnp.sum(
        jnp.where(expert_ids[..., None] == experts, gate_probs[..., None], 0.0), 1
    )
    all_tokens = lax.all_gather(tokens, BOTH, axis=0, tiled=True)
    all_dense = lax.all_gather(dense, BOTH, axis=0, tiled=True)
    load = planned_load(
        jnp.sum(all_dense, 0), swap_slot, per_device, owners, all_tokens.shape[0]
    )
    mine = lax.dynamic_slice_in_dim(
        all_dense, lax.axis_index("expert") * per_device, per_device, 1
    )
    parts = []
    for s in range(per_device):
        both = jnp.dot(all_tokens, in_weight[s], preferred_element_type=jnp.float32)
        hidden = jax.nn.silu(both[:, :half]) * both[:, half:] * mine[:, s : s + 1]
        parts.append(hidden.astype(jnp.bfloat16))
    mixed = jnp.dot(
        jnp.concatenate(parts, 1),
        out_weight.reshape(per_device * half, width),
        preferred_element_type=jnp.float32,
    ).astype(jnp.bfloat16)
    out = lax.psum_scatter(mixed, BOTH, scatter_dimension=0, tiled=True)
    return out, load


def solution(mesh):
    return jax.shard_map(
        on_device,
        mesh=mesh,
        in_specs=(
            P(BOTH, None),
            P(BOTH, None),
            P(BOTH, None),
            P("expert", None, "dp"),
            P("expert", "dp", None),
            P(),
        ),
        out_specs=(P(BOTH, None), P()),
        check_vma=False,
    )
```

profile of v0, /device:TPU:6, one launch (start us, length us, event | category | flops | bytes accessed | tf_op | source)
XLA Modules:
  0.0 2044.4 jit_solution(17175509425682315164)
XLA Ops:
  9.8 336.8 %all-gather.1 = f32[256,12,64]{2,1,0:T(8,128)} all-gather(f32[1,12,64]{2,1,0:T(8,128)S(1)} %bitcast.14), channel_id=1, replica_groups=mesh['dp'=8,'expert'=32] {'dp','expert'}, dimensions={0}, use_global_device_ids=true | all-gather | bytes 789504 | tf_op jit(solution)/shard_map/all_gather | solution.py:28
  352.7 104.2 %all-gather.4.cloned.1.call-done = bf16[256,12,4096]{2,1,0:T(8,128)(2,1)} async-done(((bf16[1,12,4096]{2,1,0:T(8,128)(2,1)}), bf16[256,12,4096]{2,1,0:T(8,128)(2,1)}) %all-gather.4.cloned.1.call-update) | async-done | bytes 25165840 | tf_op jit(solution)/shard_map/all_gather | solution.py:27
  457.0 34.8 %reshape.54 = bf16[3072,4096]{1,0:T(8,128)(2,1)} reshape(bf16[256,12,4096]{2,1,0:T(8,128)(2,1)} %all-gather.4.cloned.1.call-done) | data formatting | bytes 50331648
  491.8 14.5 fusion.1
  506.3 16.3 fusion.3
  526.8 18.4 convolution_convert_fusion
  545.3 661.3 %fusion = bf16[16,4096]{1,0:T(8,128)(2,1)S(1)} fusion(bf16[3072,4096]{1,0:T(8,128)(2,1)} %convolution_convert_fusion), kind=kCustom, calls=%all-reduce-scatter | all-reduce-scatter fusion | flops 16777216 | bytes 25296896
  1206.6 77.1 %collective-permute-start.62 = (bf16[16,4096]{1,0:T(8,128)(2,1)S(1)}, bf16[16,4096]{1,0:T(8,128)(2,1)S(1)}, u32[]{:S(2)}, u32[]{:S(2)}) collective-permute-start(bf16[16,4096]{1,0:T(8,128)(2,1)S(1)} %fusion), channel_id=1, source_target_pairs={{0,63},{1,64},{2,65},{3,66},{4,67},{5,68},{6,69},{7,70},{8,71},{9,... | collective-permute-start | bytes 393224
  1311.1 25.9 %collective-permute-done.57 = bf16[16,4096]{1,0:T(8,128)(2,1)S(1)} collective-permute-done((bf16[16,4096]{1,0:T(8,128)(2,1)S(1)}, bf16[16,4096]{1,0:T(8,128)(2,1)S(1)}, u32[]{:S(2)}, u32[]{:S(2)}) %collective-permute-start.57) | collective-permute-done | bytes 131104
  1338.9 16.6 collective-permute-done.56
  1392.9 16.0 collective-permute-done.45
  1468.1 22.1 %collective-permute-start.28 = (bf16[16,4096]{1,0:T(8,128)(2,1)S(1)}, bf16[16,4096]{1,0:T(8,128)(2,1)S(1)}, u32[]{:S(2)}, u32[]{:S(2)}) collective-permute-start(bf16[16,4096]{1,0:T(8,128)(2,1)S(1)} %fusion), channel_id=1, source_target_pairs={{0,29},{1,30},{2,31},{3,32},{4,33},{5,34},{6,35},{7,36},{8,37},{9,... | collective-permute-start | bytes 393224
  1556.0 13.1 collective-permute-start.22
  1569.1 13.1 collective-permute-start.21
  1582.3 13.1 collective-permute-start.20
  1595.4 13.1 collective-permute-start.19
  1608.6 13.1 collective-permute-start.18
  1648.0 13.1 collective-permute-start.15
  1674.3 13.1 collective-permute-start.13
  1687.4 13.1 collective-permute-start.12
  1714.1 13.1 collective-permute-start.10
  1741.7 13.1 collective-permute-start.8
  1781.1 13.1 collective-permute-start.5
  1872.4 163.5 %concatenate.4 = bf16[1036,4096]{1,0:T(8,128)(2,1)} concatenate(bf16[12,4096]{1,0:T(8,128)(2,1)} %copy-done.2, bf16[16,4096]{1,0:T(8,128)(2,1)S(1)} %collective-permute-done.62, bf16[16,4096]{1,0:T(8,128)(2,1)S(1)} %collective-permute-done.61, bf16[16,4096]{1,0:T(8,128)(2,1)} %copy-done.1, bf16[16,4096]{1,0:T(8,128)(2,1)} %copy-done.3, bf16[16,4096]{1,0:T(8,128)(2,1)} %copy-done.4, ...), dimensions={0} | concatenate | bytes 16973824
  (216 shorter events, 377.0 us)
Async XLA Ops:
  7.2 449.8 %all-gather.4.cloned.1.call-start = ((), (), s32[]{:S(2)}) async-start(), calls=%async_computation | async-start | bytes 33685504 | tf_op jit(solution)/shard_map/all_gather | solution.py:27
  1206.6 93.4 %collective-permute-start.62 = (bf16[16,4096]{1,0:T(8,128)(2,1)S(1)}, bf16[16,4096]{1,0:T(8,128)(2,1)S(1)}, u32[]{:S(2)}, u32[]{:S(2)}) collective-permute-start(bf16[16,4096]{1,0:T(8,128)(2,1)S(1)} %fusion), channel_id=1, source_target_pairs={{0,63},{1,64},{2,65},{3,66},{4,67},{5,68},{6,69},{7,70},{8,71},{9,... | collective-permute-start | bytes 393224
  1460.5 69.1 %collective-permute-start.29 = (bf16[16,4096]{1,0:T(8,128)(2,1)S(1)}, bf16[16,4096]{1,0:T(8,128)(2,1)S(1)}, u32[]{:S(2)}, u32[]{:S(2)}) collective-permute-start(bf16[16,4096]{1,0:T(8,128)(2,1)S(1)} %fusion), channel_id=1, source_target_pairs={{0,30},{1,31},{2,32},{3,33},{4,34},{5,35},{6,36},{7,37},{8,38},{9,... | collective-permute-start | bytes 393224
  1468.1 74.7 %collective-permute-start.28 = (bf16[16,4096]{1,0:T(8,128)(2,1)S(1)}, bf16[16,4096]{1,0:T(8,128)(2,1)S(1)}, u32[]{:S(2)}, u32[]{:S(2)}) collective-permute-start(bf16[16,4096]{1,0:T(8,128)(2,1)S(1)} %fusion), channel_id=1, source_target_pairs={{0,29},{1,30},{2,31},{3,32},{4,33},{5,34},{6,35},{7,36},{8,37},{9,... | collective-permute-start | bytes 393224
  1490.2 65.7 %collective-permute-start.27 = (bf16[16,4096]{1,0:T(8,128)(2,1)S(1)}, bf16[16,4096]{1,0:T(8,128)(2,1)S(1)}, u32[]{:S(2)}, u32[]{:S(2)}) collective-permute-start(bf16[16,4096]{1,0:T(8,128)(2,1)S(1)} %fusion), channel_id=1, source_target_pairs={{0,28},{1,29},{2,30},{3,31},{4,32},{5,33},{6,34},{7,35},{8,36},{9,... | collective-permute-start | bytes 393224
  1503.4 65.7 %collective-permute-start.26 = (bf16[16,4096]{1,0:T(8,128)(2,1)S(1)}, bf16[16,4096]{1,0:T(8,128)(2,1)S(1)}, u32[]{:S(2)}, u32[]{:S(2)}) collective-permute-start(bf16[16,4096]{1,0:T(8,128)(2,1)S(1)} %fusion), channel_id=1, source_target_pairs={{0,27},{1,28},{2,29},{3,30},{4,31},{5,32},{6,33},{7,34},{8,35},{9,... | collective-permute-start | bytes 393224
  1516.5 65.7 %collective-permute-start.25 = (bf16[16,4096]{1,0:T(8,128)(2,1)S(1)}, bf16[16,4096]{1,0:T(8,128)(2,1)S(1)}, u32[]{:S(2)}, u32[]{:S(2)}) collective-permute-start(bf16[16,4096]{1,0:T(8,128)(2,1)S(1)} %fusion), channel_id=1, source_target_pairs={{0,26},{1,27},{2,28},{3,29},{4,30},{5,31},{6,32},{7,33},{8,34},{9,... | collective-permute-start | bytes 393224
  1529.7 65.7 %collective-permute-start.24 = (bf16[16,4096]{1,0:T(8,128)(2,1)S(1)}, bf16[16,4096]{1,0:T(8,128)(2,1)S(1)}, u32[]{:S(2)}, u32[]{:S(2)}) collective-permute-start(bf16[16,4096]{1,0:T(8,128)(2,1)S(1)} %fusion), channel_id=1, source_target_pairs={{0,25},{1,26},{2,27},{3,28},{4,29},{5,30},{6,31},{7,32},{8,33},{9,... | collective-permute-start | bytes 393224
  1542.8 65.7 %collective-permute-start.23 = (bf16[16,4096]{1,0:T(8,128)(2,1)S(1)}, bf16[16,4096]{1,0:T(8,128)(2,1)S(1)}, u32[]{:S(2)}, u32[]{:S(2)}) collective-permute-start(bf16[16,4096]{1,0:T(8,128)(2,1)S(1)} %fusion), channel_id=1, source_target_pairs={{0,24},{1,25},{2,26},{3,27},{4,28},{5,29},{6,30},{7,31},{8,32},{9,... | collective-permute-start | bytes 393224
  1556.0 65.7 %collective-permute-start.22 = (bf16[16,4096]{1,0:T(8,128)(2,1)S(1)}, bf16[16,4096]{1,0:T(8,128)(2,1)}, u32[]{:S(2)}, u32[]{:S(2)}) collective-permute-start(bf16[16,4096]{1,0:T(8,128)(2,1)S(1)} %fusion), channel_id=1, source_target_pairs={{0,23},{1,24},{2,25},{3,26},{4,27},{5,28},{6,29},{7,30},{8,31},{9,... | collective-permute-start | bytes 393224
  1569.1 65.7 %collective-permute-start.21 = (bf16[16,4096]{1,0:T(8,128)(2,1)S(1)}, bf16[16,4096]{1,0:T(8,128)(2,1)}, u32[]{:S(2)}, u32[]{:S(2)}) collective-permute-start(bf16[16,4096]{1,0:T(8,128)(2,1)S(1)} %fusion), channel_id=1, source_target_pairs={{0,22},{1,23},{2,24},{3,25},{4,26},{5,27},{6,28},{7,29},{8,30},{9,... | collective-permute-start | bytes 393224
  1582.3 65.7 %collective-permute-start.20 = (bf16[16,4096]{1,0:T(8,128)(2,1)S(1)}, bf16[16,4096]{1,0:T(8,128)(2,1)}, u32[]{:S(2)}, u32[]{:S(2)}) collective-permute-start(bf16[16,4096]{1,0:T(8,128)(2,1)S(1)} %fusion), channel_id=1, source_target_pairs={{0,21},{1,22},{2,23},{3,24},{4,25},{5,26},{6,27},{7,28},{8,29},{9,... | collective-permute-start | bytes 393224
  1595.4 65.7 %collective-permute-start.19 = (bf16[16,4096]{1,0:T(8,128)(2,1)S(1)}, bf16[16,4096]{1,0:T(8,128)(2,1)}, u32[]{:S(2)}, u32[]{:S(2)}) collective-permute-start(bf16[16,4096]{1,0:T(8,128)(2,1)S(1)} %fusion), channel_id=1, source_target_pairs={{0,20},{1,21},{2,22},{3,23},{4,24},{5,25},{6,26},{7,27},{8,28},{9,... | collective-permute-start | bytes 393224
  1661.2 67.4 %collective-permute-start.14 = (bf16[16,4096]{1,0:T(8,128)(2,1)S(1)}, bf16[16,4096]{1,0:T(8,128)(2,1)}, u32[]{:S(2)}, u32[]{:S(2)}) collective-permute-start(bf16[16,4096]{1,0:T(8,128)(2,1)S(1)} %fusion), channel_id=1, source_target_pairs={{0,15},{1,16},{2,17},{3,18},{4,19},{5,20},{6,21},{7,22},{8,23},{9,... | collective-permute-start | bytes 393224
  1674.3 67.4 %collective-permute-start.13 = (bf16[16,4096]{1,0:T(8,128)(2,1)S(1)}, bf16[16,4096]{1,0:T(8,128)(2,1)}, u32[]{:S(2)}, u32[]{:S(2)}) collective-permute-start(bf16[16,4096]{1,0:T(8,128)(2,1)S(1)} %fusion), channel_id=1, source_target_pairs={{0,14},{1,15},{2,16},{3,17},{4,18},{5,19},{6,20},{7,21},{8,22},{9,... | collective-permute-start | bytes 393224
  1687.4 67.4 %collective-permute-start.12 = (bf16[16,4096]{1,0:T(8,128)(2,1)S(1)}, bf16[16,4096]{1,0:T(8,128)(2,1)}, u32[]{:S(2)}, u32[]{:S(2)}) collective-permute-start(bf16[16,4096]{1,0:T(8,128)(2,1)S(1)} %fusion), channel_id=1, source_target_pairs={{0,13},{1,14},{2,15},{3,16},{4,17},{5,18},{6,19},{7,20},{8,21},{9,... | collective-permute-start | bytes 393224
  1700.6 67.4 %collective-permute-start.11 = (bf16[16,4096]{1,0:T(8,128)(2,1)S(1)}, bf16[16,4096]{1,0:T(8,128)(2,1)}, u32[]{:S(2)}, u32[]{:S(2)}) collective-permute-start(bf16[16,4096]{1,0:T(8,128)(2,1)S(1)} %fusion), channel_id=1, source_target_pairs={{0,12},{1,13},{2,14},{3,15},{4,16},{5,17},{6,18},{7,19},{8,20},{9,... | collective-permute-start | bytes 393224
  1714.1 67.0 %collective-permute-start.10 = (bf16[16,4096]{1,0:T(8,128)(2,1)S(1)}, bf16[16,4096]{1,0:T(8,128)(2,1)}, u32[]{:S(2)}, u32[]{:S(2)}) collective-permute-start(bf16[16,4096]{1,0:T(8,128)(2,1)S(1)} %fusion), channel_id=1, source_target_pairs={{0,11},{1,12},{2,13},{3,14},{4,15},{5,16},{6,17},{7,18},{8,19},{9,... | collective-permute-start | bytes 393224
  1728.6 68.6 %collective-permute-start.9 = (bf16[16,4096]{1,0:T(8,128)(2,1)S(1)}, bf16[16,4096]{1,0:T(8,128)(2,1)}, u32[]{:S(2)}, u32[]{:S(2)}) collective-permute-start(bf16[16,4096]{1,0:T(8,128)(2,1)S(1)} %fusion), channel_id=1, source_target_pairs={{0,10},{1,11},{2,12},{3,13},{4,14},{5,15},{6,16},{7,17},{8,18},{9,... | collective-permute-start | bytes 393224
  1741.7 68.6 %collective-permute-start.8 = (bf16[16,4096]{1,0:T(8,128)(2,1)S(1)}, bf16[16,4096]{1,0:T(8,128)(2,1)}, u32[]{:S(2)}, u32[]{:S(2)}) collective-permute-start(bf16[16,4096]{1,0:T(8,128)(2,1)S(1)} %fusion), channel_id=1, source_target_pairs={{0,9},{1,10},{2,11},{3,12},{4,13},{5,14},{6,15},{7,16},{8,17},{9,1... | collective-permute-start | bytes 393224
  1754.9 68.6 %collective-permute-start.7 = (bf16[16,4096]{1,0:T(8,128)(2,1)S(1)}, bf16[16,4096]{1,0:T(8,128)(2,1)}, u32[]{:S(2)}, u32[]{:S(2)}) collective-permute-start(bf16[16,4096]{1,0:T(8,128)(2,1)S(1)} %fusion), channel_id=1, source_target_pairs={{0,8},{1,9},{2,10},{3,11},{4,12},{5,13},{6,14},{7,15},{8,16},{9,17... | collective-permute-start | bytes 393224
  1768.0 68.6 %collective-permute-start.6 = (bf16[16,4096]{1,0:T(8,128)(2,1)S(1)}, bf16[16,4096]{1,0:T(8,128)(2,1)}, u32[]{:S(2)}, u32[]{:S(2)}) collective-permute-start(bf16[16,4096]{1,0:T(8,128)(2,1)S(1)} %fusion), channel_id=1, source_target_pairs={{0,7},{1,8},{2,9},{3,10},{4,11},{5,12},{6,13},{7,14},{8,15},{9,16}... | collective-permute-start | bytes 393224
  1781.1 68.6 %collective-permute-start.5 = (bf16[16,4096]{1,0:T(8,128)(2,1)S(1)}, bf16[16,4096]{1,0:T(8,128)(2,1)}, u32[]{:S(2)}, u32[]{:S(2)}) collective-permute-start(bf16[16,4096]{1,0:T(8,128)(2,1)S(1)} %fusion), channel_id=1, source_target_pairs={{0,6},{1,7},{2,8},{3,9},{4,10},{5,11},{6,12},{7,13},{8,14},{9,15},... | collective-permute-start | bytes 393224
  1797.2 66.2 %collective-permute-start.4 = (bf16[16,4096]{1,0:T(8,128)(2,1)S(1)}, bf16[16,4096]{1,0:T(8,128)(2,1)S(1)}, u32[]{:S(2)}, u32[]{:S(2)}) collective-permute-start(bf16[16,4096]{1,0:T(8,128)(2,1)S(1)} %fusion), channel_id=1, source_target_pairs={{0,5},{1,6},{2,7},{3,8},{4,9},{5,10},{6,11},{7,12},{8,13},{9,14},{... | collective-permute-start | bytes 393224
  (85 other events, 12899.7 us)
Sparse Core Ops, SparseCore 0:
  9.9 447.0 all-gather.3
where the time goes:
time: 2050 us; the launch traced here: 2040 us
  blocking collectives  998 us (49%)
  starting transfers between devices  531 us (26%)
  waiting for transfers between devices  232 us (11%)
  local copies, waits for them, and re-layouts  211 us (10%)
  matrix products  49.2 us (2%)
    unnamed x1, blocking collectives  661 us
    unnamed x64, starting transfers between devices  531 us
    all_gather x1, blocking collectives, on_device(): all_dense = lax.all_gather(dense, BOTH, axis=0, tiled=True)  337 us
    unnamed x95, local copies, waits for them, and re-layouts  206 us
    unnamed x65, waiting for transfers between devices  128 us
    all_gather x1, waiting for transfers between devices, on_device(): all_tokens = lax.all_gather(tokens, BOTH, axis=0, tiled=True)  104 us
  transfers between devices with their start and end apart: 65, of which 22 were waited for; matrix products, arithmetic and copies ran while one was open for 1% of the time, Pallas kernels for 0%

commit v1 on v0

v1 whole, which is shorter than its diff:
```python
import jax
import jax.numpy as jnp
from jax import lax
from jax.experimental import pallas as pl
from jax.experimental.pallas import tpu as pltpu
from jax.sharding import PartitionSpec as P

MESH = pl.DeviceIdType.MESH
BOTH = ("dp", "expert")
NX, NYH, NYL, NZ = 4, 2, 2, 8
NY = NYH * NYL
TILE = 16
GATES = 128
BF, F32 = jnp.bfloat16, jnp.float32


def coordinates():
    dp, ex = lax.axis_index("dp"), lax.axis_index("expert")
    x, yh = dp // NYH, dp % NYH
    core, zy = ex % 2, ex // 2
    return x, yh * NYL + zy % NYL, zy // NYL, core


class Part:
    def __init__(self, at, ring, quad, mid, refs, sems):
        self.at, self.ring, self.quad, self.mid = at, ring, quad, mid
        self.n, self.nq, self.m = ring[1], quad[1], mid[1]
        self.r = TILE * self.m
        self.T, self.ACC, self.SP, self.ST, self.S1, self.S4, self.SUM4, self.S5, self.SUM5, self.S6 = refs
        self.sems = sems


def part_scratch(n, nq, m, width):
    r, q = TILE * m, width // nq
    shapes = [
        (2, n, r, width + GATES),
        (n, r, width),
        (2, r, width),
        (nq, TILE, q + GATES),
        (r, q + GATES),
        (nq, r, q),
        (r, q),
        (m, TILE, q),
        (TILE, q),
        (TILE, width),
    ]
    counts = [nq, m, nq, n, n + 1, n + 1, nq, m, nq]
    sems = [pltpu.SemaphoreType.DMA((c,)) for c in counts for _ in range(2)]
    sems += [pltpu.SemaphoreType.DMA((n + 1, 4)) for _ in range(2)]
    sems += [pltpu.SemaphoreType.REGULAR]
    return [pltpu.VMEM(s, BF) for s in shapes], sems


NBUF, NSEM = 10, 21


def kernel(x_ref, w1_hbm, w2_hbm, out_ref, mass_ref, *scratch):
    x, y, z, core = coordinates()
    sib_core = 1 - core
    d = 1 - 2 * core
    ex, dp = lax.axis_index("expert"), lax.axis_index("dp")
    width = out_ref.shape[2]
    half = w1_hbm.shape[2] // 2

    def dev(ax, i):
        if ax == "x":
            return (i * NYH + y // NYL, ex)
        if ax == "y":
            return (x * NYH + i // NYL, (z * NYL + i % NYL) * 2 + core)
        return (dp, (i * NYL + y % NYL) * 2 + core)

    sib = (dp, ex + d)
    axes = {"x": (x, NX, "x"), "y": (y, NY, "y"), "z": (z, NZ, "z")}
    specs = [("z", "y", "x"), ("x", "y", "z"), ("y", "x", "z")]
    parts = []
    for p, (a, b, c) in enumerate(specs):
        refs = scratch[p * NBUF : (p + 1) * NBUF]
        sems = scratch[3 * NBUF + p * NSEM : 3 * NBUF + (p + 1) * NSEM]
        parts.append(Part(p, axes[a], axes[b], axes[c], refs, sems))
    W1, W2, BOTHS, H, WSEM = scratch[3 * (NBUF + NSEM) :]

    loads = []
    for s in range(2):
        loads.append(
            pltpu.make_async_copy(
                w1_hbm.at[s], W1.at[:, pl.ds(s * 2 * half, 2 * half)], WSEM.at[s]
            )
        )
    loads.append(pltpu.make_async_copy(w2_hbm, W2, WSEM.at[2]))
    for load in loads:
        load.start()

    barrier = pltpu.get_barrier_semaphore()
    count = 1
    pl.semaphore_signal(barrier, inc=1, device_id=sib, device_id_type=MESH)
    for ax in "xyz":
        me, n, _ = axes[ax]
        for s in range(1, n):
            pl.semaphore_signal(
                barrier, inc=1, device_id=dev(ax, (me + s) % n), device_id_type=MESH
            )
            count += 1
    pl.semaphore_wait(barrier, count)

    def send(src, dst, ssem, rsem, to):
        pltpu.make_async_remote_copy(
            src_ref=src, dst_ref=dst, send_sem=ssem, recv_sem=rsem, device_id=to, device_id_type=MESH
        ).start()

    def got(dst, sem):
        pltpu.make_async_remote_copy(
            src_ref=dst, dst_ref=dst, send_sem=sem, recv_sem=sem, device_id=sib, device_id_type=MESH
        ).wait_recv()

    def sent(src, sem):
        pltpu.make_async_remote_copy(
            src_ref=src, dst_ref=src, send_sem=sem, recv_sem=sem, device_id=sib, device_id_type=MESH
        ).wait_send()

    def block(i, size):
        return pl.ds(pl.multiple_of(i * size, size), size)

    for p in parts:
        me, n, ax = p.quad
        piece = p.ST.shape[2]
        for s in range(1, n):
            to = (me + s) % n
            send(x_ref.at[p.at, :, block(to, piece)], p.ST.at[me], p.sems[0].at[s], p.sems[1].at[s], dev(ax, to))
    for p in parts:
        me, n, ax = p.quad
        piece = p.ST.shape[2]
        total = x_ref[p.at, :, block(me, piece)].astype(F32)
        for s in range(1, n):
            slot = (me + n - s) % n
            got(p.ST.at[slot], p.sems[1].at[s])
            total = total + p.ST[slot].astype(F32)
        mid, m, max_ = p.mid
        rows = block(mid, TILE)
        p.S1[rows, :] = total.astype(BF)
        for s in range(1, m):
            send(p.S1.at[rows], p.S1.at[rows], p.sems[2].at[s], p.sems[3].at[s], dev(max_, (mid + s) % m))
    for p in parts:
        mid, m, _ = p.mid
        for s in range(1, m):
            got(p.S1.at[block((mid + m - s) % m, TILE)], p.sems[3].at[s])
        me, n, ax = p.quad
        q = width // n
        mine = p.T.at[core, p.ring[0]]
        for s in range(1, n):
            send(p.S1.at[:, pl.ds(0, q)], mine.at[:, block(me, q)], p.sems[4].at[s], p.sems[5].at[s], dev(ax, (me + s) % n))
        p.T[core, p.ring[0], :, block(me, q)] = p.S1[:, :q]
        p.T[core, p.ring[0], :, width:] = p.S1[:, q:]

    def own_chunk(p, t):
        return (p.ring[0] + p.n - d * t) % p.n

    def sib_chunk(p, t):
        return (p.ring[0] + p.n + d * t) % p.n

    def next_dev(p):
        return dev(p.ring[2], (p.ring[0] + p.n + d) % p.n)


    for p in parts:
        me, n, ax = p.quad
        q = width // n
        for s in range(1, n):
            got(p.T.at[core, p.ring[0], :, block((me + n - s) % n, q)], p.sems[5].at[s])
        chunk = p.T.at[core, p.ring[0]]
        send(chunk, chunk, p.sems[6].at[0], p.sems[7].at[0], next_dev(p))
        send(chunk, chunk, p.sems[8].at[p.n], p.sems[9].at[p.n], sib)

    for load in loads:
        load.wait()

    tiles = 4
    tile = width // tiles
    lane = lax.broadcasted_iota(jnp.int32, (1, GATES), 1)
    experts_all = GATES // 2

    def step(p, t):
        n, r = p.n, p.r
        jo, js = own_chunk(p, t), sib_chunk(p, t)

        @pl.when(t < n)
        def _():
            chunk = p.T.at[core, jo]
            got(chunk, p.sems[7].at[t - 1])

            @pl.when(t < n - 1)
            def _():
                send(chunk, chunk, p.sems[6].at[t], p.sems[7].at[t], next_dev(p))

            send(chunk, chunk, p.sems[8].at[t], p.sems[9].at[t], sib)

        got(p.T.at[sib_core, js], p.sems[9].at[t])
        rows = jnp.concatenate([p.T[core, jo, :, :width], p.T[sib_core, js, :, :width]], 0)
        BOTHS[: 2 * r] = jnp.dot(rows, W1[...], preferred_element_type=F32)
        gates = jnp.concatenate([p.T[core, jo, :, width:], p.T[sib_core, js, :, width:]], 0).astype(F32)
        g = []
        for s in range(2):
            e = 2 * ex + s
            pick = (lane == e) | (lane == e + experts_all)
            g.append(jnp.sum(jnp.where(pick, gates, 0.0), 1, keepdims=True))
        first, second = BOTHS[: 2 * r, : 2 * half], BOTHS[: 2 * r, 2 * half :]
        low = lax.broadcasted_iota(jnp.int32, (1, 2 * half), 1) < half
        gate = jnp.where(low, first, pltpu.roll(second, half, 1))
        up = jnp.where(low, pltpu.roll(first, half, 1), second)
        hidden = jax.nn.silu(gate) * up * jnp.where(low, g[0], g[1])
        H[: 2 * r] = hidden.astype(BF)

        def other(j, _):
            cols = block(j, tile)
            p.T[sib_core, js, :, cols] = jnp.dot(
                H[r : 2 * r], W2[:, cols], preferred_element_type=F32
            ).astype(BF)
            return 0

        lax.fori_loop(0, tiles, other, 0)

        slot = t % 2

        @pl.when(t >= 3)
        def _():
            pl.semaphore_wait(p.sems[20], 1)

        send(p.T.at[sib_core, js, :, pl.ds(0, width)], p.SP.at[slot], p.sems[10].at[t], p.sems[11].at[t], sib)
        got(p.SP.at[slot], p.sems[11].at[t])

        def mine(j, _):
            cols = block(j, tile)
            total = jnp.dot(H[:r], W2[:, cols], preferred_element_type=F32) + p.SP[slot, :, cols].astype(F32)
            here = p.ACC.at[t - 1, :, cols]

            @pl.when(t == 1)
            def _():
                here[...] = total.astype(BF)

            @pl.when(t > 1)
            def _():
                got(here, p.sems[19].at[t - 1, j])
                here[...] = (total + here[...].astype(F32)).astype(BF)

            @pl.when(t < n)
            def _():
                send(here, p.ACC.at[t, :, cols], p.sems[18].at[t, j], p.sems[19].at[t, j], next_dev(p))

            return 0

        lax.fori_loop(0, tiles, mine, 0)

        @pl.when(t <= n - 2)
        def _():
            pl.semaphore_signal(p.sems[20], inc=1, device_id=sib, device_id_type=MESH)

    rounds = max(p.n for p in parts)

    def round_(k, _):
        for p in parts:
            every = rounds // p.n
            if every == 1:
                step(p, k)
            else:

                @pl.when(k % every == 0)
                def _(p=p, every=every):
                    step(p, k // every)

        return 0

    lax.fori_loop(1, rounds + 1, round_, 0)

    for p in parts:
        me, n, ax = p.quad
        q = width // n
        for s in range(1, n):
            to = (me + s) % n
            send(p.ACC.at[p.n - 1, :, block(to, q)], p.S4.at[me], p.sems[12].at[s], p.sems[13].at[s], dev(ax, to))
    for p in parts:
        me, n, ax = p.quad
        q = width // n
        total = p.ACC[p.n - 1, :, block(me, q)].astype(F32)
        for s in range(1, n):
            slot = (me + n - s) % n
            got(p.S4.at[slot], p.sems[13].at[s])
            total = total + p.S4[slot].astype(F32)
        p.SUM4[...] = total.astype(BF)
        mid, m, max_ = p.mid
        for s in range(1, m):
            to = (mid + s) % m
            send(p.SUM4.at[block(to, TILE)], p.S5.at[mid], p.sems[14].at[s], p.sems[15].at[s], dev(max_, to))
    for p in parts:
        mid, m, _ = p.mid
        total = p.SUM4[block(mid, TILE), :].astype(F32)
        for s in range(1, m):
            slot = (mid + m - s) % m
            got(p.S5.at[slot], p.sems[15].at[s])
            total = total + p.S5[slot].astype(F32)
        p.SUM5[...] = total.astype(BF)
        me, n, ax = p.quad
        q = width // n
        for s in range(1, n):
            send(p.SUM5, p.S6.at[:, block(me, q)], p.sems[16].at[s], p.sems[17].at[s], dev(ax, (me + s) % n))
        p.S6[:, block(me, q)] = p.SUM5[...]

    mass = jnp.zeros((TILE, GATES), F32)
    for p in parts:

        def add(i, m_, p=p):
            rows = p.T[i // p.n, i % p.n, :, width:].astype(F32)
            for j in range(p.m):
                m_ = m_ + rows[j * TILE : (j + 1) * TILE]
            return m_

        mass = lax.fori_loop(0, 2 * p.n, add, mass)
    mass_ref[...] = mass

    for p in parts:
        me, n, _ = p.quad
        q = width // n
        for s in range(1, n):
            got(p.S6.at[:, block((me + n - s) % n, q)], p.sems[17].at[s])
        out_ref[p.at] = p.S6[...]

    for p in parts:
        q = width // p.nq
        for s in range(1, p.nq):
            sent(p.ST.at[0], p.sems[0].at[s])
            sent(p.S1.at[:, pl.ds(0, q)], p.sems[4].at[s])
            sent(p.S4.at[0], p.sems[12].at[s])
            sent(p.SUM5, p.sems[16].at[s])
        for s in range(1, p.m):
            sent(p.S1.at[pl.ds(0, TILE)], p.sems[2].at[s])
            sent(p.S5.at[0], p.sems[14].at[s])

        def ring_sent(t, _, p=p):
            chunk = p.T.at[core, 0]

            @pl.when(t < p.n)
            def _():
                sent(chunk, p.sems[6].at[t - 1])
                for j in range(tiles):
                    sent(p.ACC.at[0, :, pl.ds(j * tile, tile)], p.sems[18].at[t, j])

            sent(chunk, p.sems[8].at[t])
            sent(p.SP.at[0], p.sems[10].at[t])
            return 0

        lax.fori_loop(1, p.n + 1, ring_sent, 0)


def fused(x, w1, w2, width):
    half = w1.shape[2] // 2
    buffers, sems = [], []
    for n, nq, m in ((NZ, NY, NX), (NX, NY, NZ), (NY, NX, NZ)):
        b, s = part_scratch(n, nq, m, width)
        buffers += b
        sems += s
    most = 2 * TILE * max(NX, NZ)
    return pl.pallas_call(
        kernel,
        out_shape=(
            jax.ShapeDtypeStruct((3, TILE, width), BF),
            jax.ShapeDtypeStruct((TILE, GATES), F32),
        ),
        in_specs=[
            pl.BlockSpec(memory_space=pltpu.VMEM),
            pl.BlockSpec(memory_space=pl.ANY),
            pl.BlockSpec(memory_space=pl.ANY),
        ],
        out_specs=(pl.BlockSpec(memory_space=pltpu.VMEM), pl.BlockSpec(memory_space=pltpu.VMEM)),
        scratch_shapes=[
            *buffers,
            *sems,
            pltpu.VMEM((width, 4 * half), BF),
            pltpu.VMEM((2 * half, width), BF),
            pltpu.VMEM((most, 4 * half), F32),
            pltpu.VMEM((most, 2 * half), BF),
            pltpu.SemaphoreType.DMA((3,)),
        ],
        compiler_params=pltpu.CompilerParams(
            collective_id=0, has_side_effects=True, vmem_limit_bytes=VMEM_LIMIT
        ),
        cost_estimate=pl.CostEstimate(flops=30_000_000_000, bytes_accessed=10_000_000, transcendentals=1_200_000),
    )(x, w1, w2)


VMEM_LIMIT = 63 * 2**20


def planned_load(mass, swap_slot, per_device, owners, tokens_all):
    experts = jnp.arange(mass.shape[0], dtype=jnp.int32)
    home, within = experts // per_device, experts % per_device
    slot = jnp.repeat(swap_slot, per_device)
    holder = jnp.where(within == slot, (home + owners // 2) % owners, home)
    hot = holder[:, None] == jnp.arange(owners, dtype=jnp.int32)
    return jnp.sum(jnp.where(hot, mass[:, None], 0.0), 0) * (owners / tokens_all)


def on_device(tokens, expert_ids, gate_probs, in_weight, out_weight, swap_slot):
    owners, groups = lax.axis_size("expert"), lax.axis_size("dp")
    per_device, width = in_weight.shape[:2]
    half = out_weight.shape[1]
    experts_all = GATES // 2
    experts = jnp.arange(experts_all, dtype=jnp.int32)
    dense = jnp.sum(
        jnp.where(expert_ids[..., None] == experts, gate_probs[..., None], 0.0), 1
    )
    high = lax.reduce_precision(dense, 8, 7)
    gates = jnp.concatenate([high, dense - high], 1).astype(BF)
    x, y, _, _ = coordinates()
    rows = tokens.shape[0] // 3
    blocks = []
    for p, (at, lines) in enumerate(((y, NY), (y, NY), (x, NX))):
        q = width // lines
        mine = slice(p * rows, (p + 1) * rows)
        wide = jnp.concatenate(
            [tokens[mine].reshape(rows, lines, q), jnp.broadcast_to(gates[mine, None], (rows, lines, GATES))], 2
        ).reshape(rows, -1)
        zero = jnp.zeros((TILE, wide.shape[1]), BF)
        blocks.append(lax.dynamic_update_slice_in_dim(zero, wide, at * rows, 0))
    mixed, mass = fused(jnp.stack(blocks), in_weight, out_weight.reshape(per_device * half, width), width)
    out = jnp.concatenate(
        [lax.dynamic_slice_in_dim(mixed[p], at * rows, rows, 0) for p, at in enumerate((y, y, x))], 0
    )
    mass = jnp.sum(mass, 0)
    mass = (mass[:experts_all] + mass[experts_all:])[: per_device * owners]
    load = planned_load(mass, swap_slot, per_device, owners, groups * owners * tokens.shape[0])
    return out, load


def solution(mesh):
    return jax.shard_map(
        on_device,
        mesh=mesh,
        in_specs=(
            P(BOTH, None),
            P(BOTH, None),
            P(BOTH, None),
            P("expert", None, "dp"),
            P("expert", "dp", None),
            P(),
        ),
        out_specs=(P(BOTH, None), P()),
        check_vma=False,
    )
```

time: 2050 us -> 223 us (0.11)
  blocking collectives: 998 us -> 0 us
  starting transfers between devices: 531 us -> 0 us
  waiting for transfers between devices: 232 us -> 0 us
  Pallas kernels: 0 us -> 214 us
  local copies, waits for them, and re-layouts: 211 us -> 4.13 us
  matrix products: 49.2 us -> 0 us
    unnamed x1 -> x0, blocking collectives: 661 us -> none
    unnamed x64 -> x0, starting transfers between devices: 531 us -> none
    all_gather x1 -> x0, blocking collectives: 337 us -> none  [on_device(): all_dense = lax.all_gather(dense, BOTH, axis=0, tiled=True)]
    pallas_call x0 -> x1, Pallas kernels: none -> 214 us  [fused(): pl.pallas_call(kernel, out_shape=(jax.ShapeDtypeStruct((3, TILE, width),...]
    unnamed x95 -> x4, local copies, waits for them, and re-layouts: 206 us -> 1.54 us
    unnamed x65 -> x0, waiting for transfers between devices: 128 us -> none
    all_gather x1 -> x0, waiting for transfers between devices: 104 us -> none  [on_device(): all_tokens = lax.all_gather(tokens, BOTH, axis=0, tiled=True)]
    dot_general x3 -> x0, matrix products: 49.2 us -> none  [the longest x2 30.8 us: on_device(): both = jnp.dot(all_tokens, in_weight[s], preferred_element_type=jnp.float32)]
  transfers between devices with their start and end apart: 65 -> 0, of which waited for: 22 -> 0; matrix products, arithmetic and copies ran while one was open for 1% -> 0% of each run, Pallas kernels for 0% -> 0%
where the time goes in v1:
time: 223 us; the launch traced here: 222 us
  Pallas kernels  214 us (96%)
  local copies, waits for them, and re-layouts  4.13 us (2%)
  other arithmetic  3.21 us (1%)
    pallas_call x1, Pallas kernels, fused(): pl.pallas_call(kernel, out_shape=(jax.ShapeDtypeStruct((3, TILE, width),...  214 us

profile of v1, /device:TPU:6, one launch (start us, length us, event | category | flops | bytes accessed | tf_op | source)
XLA Modules:
  0.0 222.2 jit_solution(7861793008858295771)
XLA Ops:
  0.7 0.8 copy.12
  1.4 0.8 copy.13
  2.2 0.1 select_reduce_fusion
  2.3 0.1 pad_maximum_fusion.7
  2.4 1.0 fusion.3
  3.9 0.8 pad_maximum_fusion.x_ref
  4.7 0.0 copy-start
  4.7 214.0 %shard_map.77 = (bf16[3,16,4096]{2,1,0:T(8,128)(2,1)}, f32[16,128]{1,0:T(8,128)}) custom-call(bf16[3,16,4608]{2,1,0:T(8,128)(2,1)} %pad_maximum_fusion.x_ref, bf16[2,4096,384]{2,1,0:T(8,128)(2,1)} %w1_hbm.1, bf16[384,4096]{1,0:T(8,128)(2,1)} %bitcast.7), custom_call_target="tpu_custom_call" | custom-call | flops 30000001024 | bytes 10000000 | tf_op jit(solution)/shard_map/pallas_call | solution.py:360
  218.7 1.1 fusion.2
  219.8 0.7 pad_maximum_fusion.1
  220.6 0.7 reduce_sum.28
  221.3 0.1 slice_add_fusion
  221.3 0.0 copy-done
  221.4 0.1 broadcast_in_dim.56
  221.4 0.1 reshape.82
  221.5 0.1 select_reduce_fusion.1
  221.7 0.5 broadcast_multiply_fusion
  (22 shorter events, 0.5 us)
Async XLA Ops:
  4.7 216.6 %copy-start = (s32[32]{0:T(128)S(1)}, s32[32]{0:T(128)}, u32[]{:S(2)}) copy-start(s32[32]{0:T(128)} %param.11) | copy-start | bytes 388

commit v2 on v1

--- a/solution.py
+++ b/solution.py
@@ -26,7 +26,7 @@
         self.at, self.ring, self.quad, self.mid = at, ring, quad, mid
         self.n, self.nq, self.m = ring[1], quad[1], mid[1]
         self.r = TILE * self.m
-        self.T, self.ACC, self.SP, self.ST, self.S1, self.S4, self.SUM4, self.S5, self.SUM5, self.S6 = refs
+        self.T, self.ACC, self.SP, self.ST, self.S1, self.S4, self.SUM4, self.S5, self.SUM5, self.S6, self.OWN = refs
         self.sems = sems
 
 
@@ -43,6 +43,7 @@
         (m, TILE, q),
         (TILE, q),
         (TILE, width),
+        (r, width),
     ]
     counts = [nq, m, nq, n, n + 1, n + 1, nq, m, nq]
     sems = [pltpu.SemaphoreType.DMA((c,)) for c in counts for _ in range(2)]
@@ -51,7 +52,7 @@
     return [pltpu.VMEM(s, BF) for s in shapes], sems
 
 
-NBUF, NSEM = 10, 21
+NBUF, NSEM = 11, 21
 
 
 def kernel(x_ref, w1_hbm, w2_hbm, out_ref, mass_ref, *scratch):
@@ -120,13 +121,24 @@
     def block(i, size):
         return pl.ds(pl.multiple_of(i * size, size), size)
 
-    for p in parts:
+    def own_chunk(p, t):
+        return (p.ring[0] + p.n - d * t) % p.n
+
+    def sib_chunk(p, t):
+        return (p.ring[0] + p.n + d * t) % p.n
+
+    def next_dev(p):
+        return dev(p.ring[2], (p.ring[0] + p.n + d) % p.n)
+
+
+    def swap_quarters(p):
         me, n, ax = p.quad
         piece = p.ST.shape[2]
         for s in range(1, n):
             to = (me + s) % n
             send(x_ref.at[p.at, :, block(to, piece)], p.ST.at[me], p.sems[0].at[s], p.sems[1].at[s], dev(ax, to))
-    for p in parts:
+
+    def gather_rows(p):
         me, n, ax = p.quad
         piece = p.ST.shape[2]
         total = x_ref[p.at, :, block(me, piece)].astype(F32)
@@ -139,7 +151,8 @@
         p.S1[rows, :] = total.astype(BF)
         for s in range(1, m):
             send(p.S1.at[rows], p.S1.at[rows], p.sems[2].at[s], p.sems[3].at[s], dev(max_, (mid + s) % m))
-    for p in parts:
+
+    def gather_quarters(p):
         mid, m, _ = p.mid
         for s in range(1, m):
             got(p.S1.at[block((mid + m - s) % m, TILE)], p.sems[3].at[s])
@@ -151,17 +164,7 @@
         p.T[core, p.ring[0], :, block(me, q)] = p.S1[:, :q]
         p.T[core, p.ring[0], :, width:] = p.S1[:, q:]
 
-    def own_chunk(p, t):
-        return (p.ring[0] + p.n - d * t) % p.n
-
-    def sib_chunk(p, t):
-        return (p.ring[0] + p.n + d * t) % p.n
-
-    def next_dev(p):
-        return dev(p.ring[2], (p.ring[0] + p.n + d) % p.n)
-
-
-    for p in parts:
+    def start_ring(p):
         me, n, ax = p.quad
         q = width // n
         for s in range(1, n):
@@ -170,6 +173,18 @@
         send(chunk, chunk, p.sems[6].at[0], p.sems[7].at[0], next_dev(p))
         send(chunk, chunk, p.sems[8].at[p.n], p.sems[9].at[p.n], sib)
 
+    A, B, C = parts
+    for p in (A, C, B):
+        swap_quarters(p)
+    for p in (A, C, B):
+        gather_rows(p)
+    gather_quarters(A)
+    start_ring(A)
+    gather_quarters(C)
+    gather_quarters(B)
+    start_ring(C)
+    start_ring(B)
+
     for load in loads:
         load.wait()
 
@@ -178,21 +193,21 @@
     lane = lax.broadcasted_iota(jnp.int32, (1, GATES), 1)
     experts_all = GATES // 2
 
-    def step(p, t):
-        n, r = p.n, p.r
-        jo, js = own_chunk(p, t), sib_chunk(p, t)
-
-        @pl.when(t < n)
-        def _():
-            chunk = p.T.at[core, jo]
+    def forward(p, t):
+        @pl.when(t < p.n)
+        def _():
+            chunk = p.T.at[core, own_chunk(p, t)]
             got(chunk, p.sems[7].at[t - 1])
 
-            @pl.when(t < n - 1)
+            @pl.when(t < p.n - 1)
             def _():
                 send(chunk, chunk, p.sems[6].at[t], p.sems[7].at[t], next_dev(p))
 
             send(chunk, chunk, p.sems[8].at[t], p.sems[9].at[t], sib)
 
+    def compute(p, t):
+        r = p.r
+        jo, js = own_chunk(p, t), sib_chunk(p, t)
         got(p.T.at[sib_core, js], p.sems[9].at[t])
         rows = jnp.concatenate([p.T[core, jo, :, :width], p.T[sib_core, js, :, :width]], 0)
         BOTHS[: 2 * r] = jnp.dot(rows, W1[...], preferred_element_type=F32)
@@ -209,36 +224,37 @@
         hidden = jax.nn.silu(gate) * up * jnp.where(low, g[0], g[1])
         H[: 2 * r] = hidden.astype(BF)
 
-        def other(j, _):
+        def down(j, _):
             cols = block(j, tile)
-            p.T[sib_core, js, :, cols] = jnp.dot(
-                H[r : 2 * r], W2[:, cols], preferred_element_type=F32
-            ).astype(BF)
+            both = jnp.dot(H[: 2 * r], W2[:, cols], preferred_element_type=F32).astype(BF)
+            p.OWN[:, cols] = both[:r]
+            p.T[sib_core, js, :, cols] = both[r:]
             return 0
 
-        lax.fori_loop(0, tiles, other, 0)
-
-        slot = t % 2
+        lax.fori_loop(0, tiles, down, 0)
 
         @pl.when(t >= 3)
         def _():
             pl.semaphore_wait(p.sems[20], 1)
 
-        send(p.T.at[sib_core, js, :, pl.ds(0, width)], p.SP.at[slot], p.sems[10].at[t], p.sems[11].at[t], sib)
+        send(p.T.at[sib_core, js, :, pl.ds(0, width)], p.SP.at[t % 2], p.sems[10].at[t], p.sems[11].at[t], sib)
+
+    def combine(p, t):
+        n, slot = p.n, t % 2
         got(p.SP.at[slot], p.sems[11].at[t])
 
-        def mine(j, _):
+        def add(j, _):
             cols = block(j, tile)
-            total = jnp.dot(H[:r], W2[:, cols], preferred_element_type=F32) + p.SP[slot, :, cols].astype(F32)
             here = p.ACC.at[t - 1, :, cols]
 
             @pl.when(t == 1)
             def _():
-                here[...] = total.astype(BF)
+                here[...] = (p.OWN[:, cols].astype(F32) + p.SP[slot, :, cols].astype(F32)).astype(BF)
 
             @pl.when(t > 1)
             def _():
                 got(here, p.sems[19].at[t - 1, j])
+                total = p.OWN[:, cols].astype(F32) + p.SP[slot, :, cols].astype(F32)
                 here[...] = (total + here[...].astype(F32)).astype(BF)
 
             @pl.when(t < n)
@@ -247,36 +263,23 @@
 
             return 0
 
-        lax.fori_loop(0, tiles, mine, 0)
+        lax.fori_loop(0, tiles, add, 0)
 
         @pl.when(t <= n - 2)
         def _():
             pl.semaphore_signal(p.sems[20], inc=1, device_id=sib, device_id_type=MESH)
 
-    rounds = max(p.n for p in parts)
-
-    def round_(k, _):
-        for p in parts:
-            every = rounds // p.n
-            if every == 1:
-                step(p, k)
-            else:
-
-                @pl.when(k % every == 0)
-                def _(p=p, every=every):
-                    step(p, k // every)
-
-        return 0
-
-    lax.fori_loop(1, rounds + 1, round_, 0)
-
-    for p in parts:
+    every = A.n // B.n
+    assert A.n == every * B.n and B.n == C.n
+
+    def reduce_quarters(p):
         me, n, ax = p.quad
         q = width // n
         for s in range(1, n):
             to = (me + s) % n
             send(p.ACC.at[p.n - 1, :, block(to, q)], p.S4.at[me], p.sems[12].at[s], p.sems[13].at[s], dev(ax, to))
-    for p in parts:
+
+    def reduce_rows(p):
         me, n, ax = p.quad
         q = width // n
         total = p.ACC[p.n - 1, :, block(me, q)].astype(F32)
@@ -289,7 +292,8 @@
         for s in range(1, m):
             to = (mid + s) % m
             send(p.SUM4.at[block(to, TILE)], p.S5.at[mid], p.sems[14].at[s], p.sems[15].at[s], dev(max_, to))
-    for p in parts:
+
+    def return_rows(p):
         mid, m, _ = p.mid
         total = p.SUM4[block(mid, TILE), :].astype(F32)
         for s in range(1, m):
@@ -302,6 +306,42 @@
         for s in range(1, n):
             send(p.SUM5, p.S6.at[:, block(me, q)], p.sems[16].at[s], p.sems[17].at[s], dev(ax, (me + s) % n))
         p.S6[:, block(me, q)] = p.SUM5[...]
+
+    def round_(k, _):
+        forward(A, every * k - 1)
+        compute(A, every * k - 1)
+        forward(B, k)
+        compute(B, k)
+        combine(A, every * k - 1)
+        forward(C, k)
+        compute(C, k)
+        combine(B, k)
+        @pl.when(k == B.n)
+        def _():
+            reduce_quarters(B)
+
+        forward(A, every * k)
+        compute(A, every * k)
+        combine(C, k)
+        @pl.when(k == B.n)
+        def _():
+            reduce_quarters(C)
+
+        combine(A, every * k)
+        @pl.when(k == B.n)
+        def _():
+            reduce_quarters(A)
+
+        return 0
+
+    lax.fori_loop(1, B.n + 1, round_, 0)
+
+    reduce_rows(B)
+    reduce_rows(C)
+    reduce_rows(A)
+    return_rows(B)
+    return_rows(C)
+    return_rows(A)
 
     mass = jnp.zeros((TILE, GATES), F32)
     for p in parts:

time: 223 us -> 194 us (0.87)
  Pallas kernels: 214 us -> 183 us
    pallas_call x1, Pallas kernels: 214 us -> 183 us  [fused(): pl.pallas_call(kernel, out_shape=(jax.ShapeDtypeStruct((3, TILE, width),...]
where the time goes in v2:
time: 194 us; the launch traced here: 191 us
  Pallas kernels  183 us (94%)
  local copies, waits for them, and re-layouts  4.13 us (2%)
  other arithmetic  3.21 us (2%)
    pallas_call x1, Pallas kernels, fused(): pl.pallas_call(kernel, out_shape=(jax.ShapeDtypeStruct((3, TILE, width),...  183 us

profile of v2, /device:TPU:6, one launch (start us, length us, event | category | flops | bytes accessed | tf_op | source)
XLA Modules:
  0.0 191.0 jit_solution(1290436510491022259)
XLA Ops:
  0.7 0.8 copy.12
  1.4 0.8 copy.13
  2.2 0.1 select_reduce_fusion
  2.3 0.1 pad_maximum_fusion.7
  2.4 1.0 fusion.3
  3.9 0.8 pad_maximum_fusion.x_ref
  4.7 0.0 copy-start
  4.7 182.7 %shard_map.77 = (bf16[3,16,4096]{2,1,0:T(8,128)(2,1)}, f32[16,128]{1,0:T(8,128)}) custom-call(bf16[3,16,4608]{2,1,0:T(8,128)(2,1)} %pad_maximum_fusion.x_ref, bf16[2,4096,384]{2,1,0:T(8,128)(2,1)} %w1_hbm.1, bf16[384,4096]{1,0:T(8,128)(2,1)} %bitcast.7), custom_call_target="tpu_custom_call" | custom-call | flops 30000001024 | bytes 10000000 | tf_op jit(solution)/shard_map/pallas_call | solution.py:400
  187.5 1.1 fusion.2
  188.6 0.7 pad_maximum_fusion.1
  189.3 0.7 reduce_sum.28
  190.0 0.1 slice_add_fusion
  190.1 0.0 copy-done
  190.1 0.1 broadcast_in_dim.56
  190.2 0.1 reshape.82
  190.3 0.1 select_reduce_fusion.1
  190.4 0.5 broadcast_multiply_fusion
  (22 shorter events, 0.5 us)
Async XLA Ops:
  4.7 185.4 %copy-start = (s32[32]{0:T(128)S(1)}, s32[32]{0:T(128)}, u32[]{:S(2)}) copy-start(s32[32]{0:T(128)} %param.11) | copy-start | bytes 388

commit v3 on v2

--- a/solution.py
+++ b/solution.py
@@ -45,8 +45,8 @@
         (TILE, width),
         (r, width),
     ]
-    counts = [nq, m, nq, n, n + 1, n + 1, nq, m, nq]
-    sems = [pltpu.SemaphoreType.DMA((c,)) for c in counts for _ in range(2)]
+    counts = [(nq,), (m,), (m, nq), (n,), (n + 1,), (n + 1,), (m, nq), (m,), (nq,)]
+    sems = [pltpu.SemaphoreType.DMA(c) for c in counts for _ in range(2)]
     sems += [pltpu.SemaphoreType.DMA((n + 1, 4)) for _ in range(2)]
     sems += [pltpu.SemaphoreType.REGULAR]
     return [pltpu.VMEM(s, BF) for s in shapes], sems
@@ -131,6 +131,9 @@
         return dev(p.ring[2], (p.ring[0] + p.n + d) % p.n)
 
 
+    def nearest(n):
+        return sorted(range(1, n), key=lambda s: min(s, n - s))
+
     def swap_quarters(p):
         me, n, ax = p.quad
         piece = p.ST.shape[2]
@@ -149,26 +152,31 @@
         mid, m, max_ = p.mid
         rows = block(mid, TILE)
         p.S1[rows, :] = total.astype(BF)
-        for s in range(1, m):
+        for s in nearest(m):
             send(p.S1.at[rows], p.S1.at[rows], p.sems[2].at[s], p.sems[3].at[s], dev(max_, (mid + s) % m))
 
     def gather_quarters(p):
         mid, m, _ = p.mid
-        for s in range(1, m):
-            got(p.S1.at[block((mid + m - s) % m, TILE)], p.sems[3].at[s])
         me, n, ax = p.quad
         q = width // n
         mine = p.T.at[core, p.ring[0]]
-        for s in range(1, n):
-            send(p.S1.at[:, pl.ds(0, q)], mine.at[:, block(me, q)], p.sems[4].at[s], p.sems[5].at[s], dev(ax, (me + s) % n))
+        for s in [0] + nearest(m):
+            rows = block((mid + m - s) % m, TILE)
+            if s:
+                got(p.S1.at[rows], p.sems[3].at[s])
+            for u in range(1, n):
+                send(p.S1.at[rows, pl.ds(0, q)], mine.at[rows, block(me, q)], p.sems[4].at[s, u], p.sems[5].at[s, u], dev(ax, (me + u) % n))
         p.T[core, p.ring[0], :, block(me, q)] = p.S1[:, :q]
         p.T[core, p.ring[0], :, width:] = p.S1[:, q:]
 
     def start_ring(p):
+        mid, m, _ = p.mid
         me, n, ax = p.quad
         q = width // n
-        for s in range(1, n):
-            got(p.T.at[core, p.ring[0], :, block((me + n - s) % n, q)], p.sems[5].at[s])
+        for s in [0] + nearest(m):
+            rows = block((mid + m - s) % m, TILE)
+            for u in range(1, n):
+                got(p.T.at[core, p.ring[0], rows, block((me + n - u) % n, q)], p.sems[5].at[s, u])
         chunk = p.T.at[core, p.ring[0]]
         send(chunk, chunk, p.sems[6].at[0], p.sems[7].at[0], next_dev(p))
         send(chunk, chunk, p.sems[8].at[p.n], p.sems[9].at[p.n], sib)
@@ -182,8 +190,6 @@
     start_ring(A)
     gather_quarters(C)
     gather_quarters(B)
-    start_ring(C)
-    start_ring(B)
 
     for load in loads:
         load.wait()
@@ -269,34 +275,38 @@
         def _():
             pl.semaphore_signal(p.sems[20], inc=1, device_id=sib, device_id_type=MESH)
 
-    every = A.n // B.n
-    assert A.n == every * B.n and B.n == C.n
+    assert A.n == 2 * B.n and B.n == C.n
 
     def reduce_quarters(p):
+        mid, m, _ = p.mid
         me, n, ax = p.quad
         q = width // n
-        for s in range(1, n):
-            to = (me + s) % n
-            send(p.ACC.at[p.n - 1, :, block(to, q)], p.S4.at[me], p.sems[12].at[s], p.sems[13].at[s], dev(ax, to))
+        for s in nearest(m)[::-1] + [0]:
+            rows = block((mid + s) % m, TILE)
+            for u in range(1, n):
+                to = (me + u) % n
+                send(p.ACC.at[p.n - 1, rows, block(to, q)], p.S4.at[me, rows], p.sems[12].at[s, u], p.sems[13].at[s, u], dev(ax, to))
 
     def reduce_rows(p):
+        mid, m, max_ = p.mid
         me, n, ax = p.quad
         q = width // n
-        total = p.ACC[p.n - 1, :, block(me, q)].astype(F32)
-        for s in range(1, n):
-            slot = (me + n - s) % n
-            got(p.S4.at[slot], p.sems[13].at[s])
-            total = total + p.S4[slot].astype(F32)
-        p.SUM4[...] = total.astype(BF)
-        mid, m, max_ = p.mid
-        for s in range(1, m):
+        for s in nearest(m)[::-1] + [0]:
             to = (mid + s) % m
-            send(p.SUM4.at[block(to, TILE)], p.S5.at[mid], p.sems[14].at[s], p.sems[15].at[s], dev(max_, to))
+            rows = block(to, TILE)
+            total = p.ACC[p.n - 1, rows, block(me, q)].astype(F32)
+            for u in range(1, n):
+                slot = (me + n - u) % n
+                got(p.S4.at[slot, rows], p.sems[13].at[s, u])
+                total = total + p.S4[slot, rows, :].astype(F32)
+            p.SUM4[rows, :] = total.astype(BF)
+            if s:
+                send(p.SUM4.at[rows], p.S5.at[mid], p.sems[14].at[s], p.sems[15].at[s], dev(max_, to))
 
     def return_rows(p):
         mid, m, _ = p.mid
         total = p.SUM4[block(mid, TILE), :].astype(F32)
-        for s in range(1, m):
+        for s in nearest(m)[::-1]:
             slot = (mid + m - s) % m
             got(p.S5.at[slot], p.sems[15].at[s])
             total = total + p.S5[slot].astype(F32)
@@ -307,41 +317,47 @@
             send(p.SUM5, p.S6.at[:, block(me, q)], p.sems[16].at[s], p.sems[17].at[s], dev(ax, (me + s) % n))
         p.S6[:, block(me, q)] = p.SUM5[...]
 
-    def round_(k, _):
-        forward(A, every * k - 1)
-        compute(A, every * k - 1)
-        forward(B, k)
-        compute(B, k)
-        combine(A, every * k - 1)
-        forward(C, k)
-        compute(C, k)
-        combine(B, k)
+    forward(A, 1)
+    start_ring(C)
+    start_ring(B)
+    compute(A, 1)
+    combine(A, 1)
+
+    def last(k, f, p):
         @pl.when(k == B.n)
         def _():
-            reduce_quarters(B)
-
-        forward(A, every * k)
-        compute(A, every * k)
+            f(p)
+
+    def odd(k, f):
+        @pl.when(k < B.n)
+        def _():
+            f(A, 2 * k + 1)
+
+    def round_(k, _):
+        forward(A, 2 * k)
+        compute(A, 2 * k)
+        forward(B, k)
+        forward(C, k)
+        combine(A, 2 * k)
+        last(k, reduce_quarters, A)
+        compute(B, k)
+        odd(k, forward)
+        combine(B, k)
+        last(k, reduce_quarters, B)
+        odd(k, compute)
+        compute(C, k)
+        odd(k, combine)
         combine(C, k)
-        @pl.when(k == B.n)
-        def _():
-            reduce_quarters(C)
-
-        combine(A, every * k)
-        @pl.when(k == B.n)
-        def _():
-            reduce_quarters(A)
-
+        last(k, reduce_quarters, C)
         return 0
 
     lax.fori_loop(1, B.n + 1, round_, 0)
-
+    reduce_rows(A)
     reduce_rows(B)
     reduce_rows(C)
-    reduce_rows(A)
+    return_rows(A)
     return_rows(B)
     return_rows(C)
-    return_rows(A)
 
     mass = jnp.zeros((TILE, GATES), F32)
     for p in parts:
@@ -366,9 +382,10 @@
         q = width // p.nq
         for s in range(1, p.nq):
             sent(p.ST.at[0], p.sems[0].at[s])
-            sent(p.S1.at[:, pl.ds(0, q)], p.sems[4].at[s])
-            sent(p.S4.at[0], p.sems[12].at[s])
             sent(p.SUM5, p.sems[16].at[s])
+            for g in range(p.m):
+                sent(p.S1.at[pl.ds(0, TILE), pl.ds(0, q)], p.sems[4].at[g, s])
+                sent(p.S4.at[0, pl.ds(0, TILE)], p.sems[12].at[g, s])
         for s in range(1, p.m):
             sent(p.S1.at[pl.ds(0, TILE)], p.sems[2].at[s])
             sent(p.S5.at[0], p.sems[14].at[s])

time: 194 us -> 173 us (0.89); the launches traced: 191 us -> 173 us
  Pallas kernels: 183 us -> 165 us
    pallas_call x1, Pallas kernels: 183 us -> 165 us  [fused(): pl.pallas_call(kernel, out_shape=(jax.ShapeDtypeStruct((3, TILE, width),...]
where the time goes in v3:
time: 173 us
  Pallas kernels  165 us (95%)
  local copies, waits for them, and re-layouts  4.13 us (2%)
  other arithmetic  3.21 us (2%)
    pallas_call x1, Pallas kernels, fused(): pl.pallas_call(kernel, out_shape=(jax.ShapeDtypeStruct((3, TILE, width),...  165 us

profile of v3, /device:TPU:6, one launch (start us, length us, event | category | flops | bytes accessed | tf_op | source)
XLA Modules:
  0.0 173.2 jit_solution(18307338194341369165)
XLA Ops:
  0.7 0.8 copy.12
  1.4 0.8 copy.13
  2.2 0.1 select_reduce_fusion
  2.3 0.1 pad_maximum_fusion.7
  2.4 1.0 fusion.3
  3.9 0.8 pad_maximum_fusion.x_ref
  4.7 0.0 copy-start
  4.7 165.0 %shard_map.77 = (bf16[3,16,4096]{2,1,0:T(8,128)(2,1)}, f32[16,128]{1,0:T(8,128)}) custom-call(bf16[3,16,4608]{2,1,0:T(8,128)(2,1)} %pad_maximum_fusion.x_ref, bf16[2,4096,384]{2,1,0:T(8,128)(2,1)} %w1_hbm.1, bf16[384,4096]{1,0:T(8,128)(2,1)} %bitcast.7), custom_call_target="tpu_custom_call" | custom-call | flops 30000001024 | bytes 10000000 | tf_op jit(solution)/shard_map/pallas_call | solution.py:417
  169.7 1.1 fusion.2
  170.9 0.7 pad_maximum_fusion.1
  171.6 0.7 reduce_sum.28
  172.3 0.1 slice_add_fusion
  172.4 0.0 copy-done
  172.4 0.1 broadcast_in_dim.56
  172.5 0.1 reshape.82
  172.6 0.1 select_reduce_fusion.1
  172.7 0.5 broadcast_multiply_fusion
  (22 shorter events, 0.5 us)
Async XLA Ops:
  4.7 167.7 %copy-start = (s32[32]{0:T(128)S(1)}, s32[32]{0:T(128)}, u32[]{:S(2)}) copy-start(s32[32]{0:T(128)} %param.11) | copy-start | bytes 388

commit v4 on v3

--- a/solution.py
+++ b/solution.py
@@ -336,25 +336,25 @@
     def round_(k, _):
         forward(A, 2 * k)
         compute(A, 2 * k)
+        forward(C, k)
         forward(B, k)
-        forward(C, k)
         combine(A, 2 * k)
         last(k, reduce_quarters, A)
+        compute(C, k)
+        odd(k, forward)
         compute(B, k)
-        odd(k, forward)
+        combine(C, k)
+        last(k, reduce_quarters, C)
+        odd(k, compute)
+        odd(k, combine)
+        last(k, reduce_rows, A)
         combine(B, k)
         last(k, reduce_quarters, B)
-        odd(k, compute)
-        compute(C, k)
-        odd(k, combine)
-        combine(C, k)
-        last(k, reduce_quarters, C)
         return 0
 
     lax.fori_loop(1, B.n + 1, round_, 0)
-    reduce_rows(A)
+    reduce_rows(C)
     reduce_rows(B)
-    reduce_rows(C)
     return_rows(A)
     return_rows(B)
     return_rows(C)

time: 173 us -> 167 us (0.965); the launches traced: 173 us -> 165 us
  Pallas kernels: 165 us -> 156 us
    pallas_call x1, Pallas kernels: 165 us -> 156 us  [fused(): pl.pallas_call(kernel, out_shape=(jax.ShapeDtypeStruct((3, TILE, width),...]
where the time goes in v4:
time: 167 us; the launch traced here: 165 us
  Pallas kernels  156 us (93%)
  local copies, waits for them, and re-layouts  4.13 us (2%)
  other arithmetic  3.21 us (2%)
    pallas_call x1, Pallas kernels, fused(): pl.pallas_call(kernel, out_shape=(jax.ShapeDtypeStruct((3, TILE, width),...  156 us

profile of v4, /device:TPU:6, one launch (start us, length us, event | category | flops | bytes accessed | tf_op | source)
XLA Modules:
  0.0 164.5 jit_solution(4888545775842654977)
XLA Ops:
  0.7 0.8 copy.12
  1.4 0.8 copy.13
  2.2 0.1 select_reduce_fusion
  2.3 0.1 pad_maximum_fusion.7
  2.4 1.0 fusion.3
  3.9 0.8 pad_maximum_fusion.x_ref
  4.7 0.0 copy-start
  4.7 156.3 %shard_map.77 = (bf16[3,16,4096]{2,1,0:T(8,128)(2,1)}, f32[16,128]{1,0:T(8,128)}) custom-call(bf16[3,16,4608]{2,1,0:T(8,128)(2,1)} %pad_maximum_fusion.x_ref, bf16[2,4096,384]{2,1,0:T(8,128)(2,1)} %w1_hbm.1, bf16[384,4096]{1,0:T(8,128)(2,1)} %bitcast.7), custom_call_target="tpu_custom_call" | custom-call | flops 30000001024 | bytes 10000000 | tf_op jit(solution)/shard_map/pallas_call | solution.py:417
  161.0 1.1 fusion.2
  162.2 0.7 pad_maximum_fusion.1
  162.9 0.7 reduce_sum.28
  163.6 0.1 slice_add_fusion
  163.7 0.0 copy-done
  163.7 0.1 broadcast_in_dim.56
  163.7 0.1 reshape.82
  163.9 0.1 select_reduce_fusion.1
  164.0 0.5 broadcast_multiply_fusion
  (22 shorter events, 0.5 us)
Async XLA Ops:
  4.7 159.0 %copy-start = (s32[32]{0:T(128)S(1)}, s32[32]{0:T(128)}, u32[]{:S(2)}) copy-start(s32[32]{0:T(128)} %param.11) | copy-start | bytes 388
